TPU v7x, 32 devices: a whole 2x2x4 slice. The times are simulated.
32 devices in a mesh: seq: 16 (over z, y, x), tp: 2 (over core).
Axes of the slice: x: 2, y: 2, z: 4, core: 2. Of those that a mesh axis runs over, the one named last changes fastest.
Arguments:
- activations: float32 [2, 1024, 1024], P(None, 'seq'), may hold values from -6 to 6
- cotangent: float32 [2, 1024, 1024], P(None, 'seq')
- segment_ids: int32 [2, 1024], P(None, 'seq'), may hold values from 0 to 7, as said below
- position_ids: int32 [2, 1024], P(None, 'seq'), may hold values from 0 to 2046, as said below
- qkv_weight: float32 [2, 1024, 3, 1024], P(None, 'seq', None, 'tp')
- out_weight: float32 [2, 1024, 1024], P(None, 'seq', 'tp')
- in_weight: float32 [2, 1024, 4096], P(None, 'seq', 'tp')
- down_weight: float32 [2, 1024, 4096], P(None, 'seq', 'tp')
- norm_params: float32 [2, 3, 1024], P(None, None, 'seq')
- qkv_first: float32 [2, 1024, 3, 1024], P(None, 'seq', None, 'tp'), may hold values from -0.4375 to 0.4375
- out_first: float32 [2, 1024, 1024], P(None, 'seq', 'tp'), may hold values from -0.4375 to 0.4375
- in_first: float32 [2, 1024, 4096], P(None, 'seq', 'tp'), may hold values from -0.4375 to 0.4375
- down_first: float32 [2, 1024, 4096], P(None, 'seq', 'tp'), may hold values from -0.4375 to 0.4375
- norm_first: float32 [2, 3, 1024], P(None, None, 'seq'), may hold values from -1.5 to 1.5
- qkv_second: float32 [2, 1024, 3, 1024], P(None, 'seq', None, 'tp'), may hold values from 6.25e-05 to 0.00025
- out_second: float32 [2, 1024, 1024], P(None, 'seq', 'tp'), may hold values from 6.25e-05 to 0.00025
- in_second: float32 [2, 1024, 4096], P(None, 'seq', 'tp'), may hold values from 2e-05 to 8e-05
- down_second: float32 [2, 1024, 4096], P(None, 'seq', 'tp'), may hold values from 6.25e-05 to 0.00025
- norm_second: float32 [2, 3, 1024], P(None, None, 'seq'), may hold values from 0.0008 to 0.0032
Outputs:
- result: float32 [2, 1024, 1024], P(None, 'seq')
- input_grad: float32 [2, 1024, 1024], P(None, 'seq')
- grad_norm: float32 [], replicated
- qkv_new: float32 [2, 1024, 3, 1024], P(None, 'seq', None, 'tp')
- out_new: float32 [2, 1024, 1024], P(None, 'seq', 'tp')
- in_new: float32 [2, 1024, 4096], P(None, 'seq', 'tp')
- down_new: float32 [2, 1024, 4096], P(None, 'seq', 'tp')
- norm_new: float32 [2, 3, 1024], P(None, None, 'seq')
- qkv_first_new: float32 [2, 1024, 3, 1024], P(None, 'seq', None, 'tp')
- out_first_new: float32 [2, 1024, 1024], P(None, 'seq', 'tp')
- in_first_new: float32 [2, 1024, 4096], P(None, 'seq', 'tp')
- down_first_new: float32 [2, 1024, 4096], P(None, 'seq', 'tp')
- norm_first_new: float32 [2, 3, 1024], P(None, None, 'seq')
- qkv_second_new: float32 [2, 1024, 3, 1024], P(None, 'seq', None, 'tp')
- out_second_new: float32 [2, 1024, 1024], P(None, 'seq', 'tp')
- in_second_new: float32 [2, 1024, 4096], P(None, 'seq', 'tp')
- down_second_new: float32 [2, 1024, 4096], P(None, 'seq', 'tp')
- norm_second_new: float32 [2, 3, 1024], P(None, None, 'seq')
- bias_clipped: float32 [2, 1024], P(None, 'seq')
Inputs may be any that keep to these rules, and one draw needn't show every extreme that they name: `segment_ids`: in every row the protein numbers start at 0 and never fall along the row; one of the 2 rows holds a single protein, every other row exactly 8 proteins. `position_ids`: within a protein the positions start at 0 and rise by 1 or 2 from one residue to the next; in the row that holds a single protein they rise by 2.
All inputs are finite; a program needn't handle non-finite values.
Results may differ from a plain program's by a relative error of at most 0.03.
The roundings to bfloat16 on the way count: a program that leaves them out, or rounds other values in their place, can miss the bound.
Values may be sent and summed in bfloat16 or wider, within the bound.
A program may use at most 192 MiB of HBM per device.

v0:
```python
import math

import jax
import jax.numpy as jnp
from jax import lax
from jax.sharding import PartitionSpec as P

HEAD = 64
ROTARY = 32
LAYERS = 2
KEY_BLOCK = 512
STEP = 10
NPARAM = 25171968


norm_eps = 1e-05
beta_one = 0.9
beta_two = 0.999
adam_eps = 1e-08
rate_matrix = 0.05
rate_output = 0.15
rate_vector = 1.0
decay_matrix = 0.1
clip_share = 0.25
low_score = -1e30


def layer_norm(inputs, gain_row, shift_row):
    average = jnp.mean(inputs, axis=-1, keepdims=True)
    centred = inputs - average
    spread = jnp.mean(centred * centred, axis=-1, keepdims=True)
    return centred * lax.rsqrt(spread + norm_eps) * gain_row + shift_row


def rotary_tables(positions, columns_total):
    column = jnp.arange(columns_total) % HEAD
    inside = column < ROTARY
    pair_index = column % ROTARY // 2
    frequency = jnp.exp(pair_index.astype(jnp.float32) * (-2.0 * math.log(10000.0) / ROTARY))
    angles = positions.astype(jnp.float32)[..., None] * frequency
    cosine = jnp.where(inside, jnp.cos(angles), 1.0)
    signed = jnp.where(column % 2 == 0, -1.0, 1.0)
    sine = jnp.where(inside, signed * jnp.sin(angles), 0.0)
    return (cosine, sine)


def swap_pairs(values):
    extent = values.shape
    paired = values.reshape(extent[:-1] + (extent[-1] // 2, 2))
    return jnp.flip(paired, axis=-1).reshape(extent)


def rotate(values, cosine, sine):
    return values * cosine + swap_pairs(values) * sine


def rotate_back(gradient, cosine, sine):
    return gradient * cosine + swap_pairs(gradient * sine)


def gelu_tanh(values):
    return jax.nn.gelu(values, approximate=True)


def split_heads(values):
    extent = values.shape
    return values.reshape(extent[:-1] + (extent[-1] // HEAD, HEAD))


def block_scores(queries, key_rows):
    return jnp.einsum(
        "rqhd,rkhd->rhqk", queries, key_rows, preferred_element_type=jnp.float32
    ) * HEAD ** (-0.5)


def allowed_mask(query_places, query_segments, key_places, key_segments):
    causal = key_places[None, None, :] <= query_places[None, :, None]
    matching = query_segments[:, :, None] == key_segments[:, None, :]
    return (causal & matching)[:, None]


def unchanged(carried):
    return carried


def key_sweep(
    block_update, carry_start, keys_all, values_all, segments_all, query_places, query_segments
):
    length = keys_all.shape[1]
    last_place = query_places[-1]

    def key_advance(carried, block_index):
        key_start = block_index * KEY_BLOCK

        def key_compute(inner):
            key_rows = lax.dynamic_slice_in_dim(keys_all, key_start, KEY_BLOCK, 1)
            value_rows = lax.dynamic_slice_in_dim(values_all, key_start, KEY_BLOCK, 1)
            key_segments = lax.dynamic_slice_in_dim(segments_all, key_start, KEY_BLOCK, 1)
            key_places = key_start + jnp.arange(KEY_BLOCK)
            allowed = allowed_mask(query_places, query_segments, key_places, key_segments)
            return block_update(inner, key_rows, value_rows, allowed, key_start)

        return (lax.cond(key_start <= last_place, key_compute, unchanged, carried), None)

    finished, unused = lax.scan(key_advance, carry_start, jnp.arange(length // KEY_BLOCK))
    return finished


def total_step(queries):

    def block_update(carried, key_rows, value_rows, allowed, key_start):
        maxima, totals = carried
        scores = jnp.where(allowed, block_scores(queries, key_rows), low_score)
        raised = jnp.maximum(maxima, jnp.max(scores, axis=-1))
        weights = jnp.where(allowed, jnp.exp(scores - raised[..., None]), 0.0)
        return (raised, totals * jnp.exp(maxima - raised) + jnp.sum(weights, axis=-1))

    return block_update


def value_step(queries, log_totals):

    def block_update(carried, key_rows, value_rows, allowed, key_start):
        shares = jnp.where(
            allowed, jnp.exp(block_scores(queries, key_rows) - log_totals[..., None]), 0.0
        )
        return carried + jnp.einsum(
            "rhqk,rkhd->rqhd",
            shares.astype(jnp.bfloat16),
            value_rows,
            preferred_element_type=jnp.float32,
        )

    return block_update


def revisit_step(queries, log_totals, head_grads):

    def block_update(carried, key_rows, value_rows, allowed, key_start):
        outputs, deltas = carried
        shares = jnp.where(
            allowed, jnp.exp(block_scores(queries, key_rows) - log_totals[..., None]), 0.0
        )
        outputs = outputs + jnp.einsum(
            "rhqk,rkhd->rqhd",
            shares.astype(jnp.bfloat16),
            value_rows,
            preferred_element_type=jnp.float32,
        )
        share_grads = jnp.einsum(
            "rqhd,rkhd->rhqk", head_grads, value_rows, preferred_element_type=jnp.float32
        )
        return (outputs, deltas + jnp.sum(shares * share_grads, axis=-1))

    return block_update


def gradient_step(queries, log_totals, head_grads, deltas):

    def block_update(carried, key_rows, value_rows, allowed, key_start):
        shares = jnp.where(
            allowed, jnp.exp(block_scores(queries, key_rows) - log_totals[..., None]), 0.0
        )
        share_grads = jnp.einsum(
            "rqhd,rkhd->rhqk", head_grads, value_rows, preferred_element_type=jnp.float32
        )
        score_grads = (shares * (share_grads - deltas[..., None])).astype(jnp.bfloat16)
        query_grads = carried[0] + jnp.einsum(
            "rhqk,rkhd->rqhd", score_grads, key_rows, preferred_element_type=jnp.float32
        )
        return (query_grads,)

    return block_update


def query_sweep(own_keys, own_values, own_segments, own_places, gathered, segments_all):
    queries_all, grads_all, totals_all, deltas_all = gathered
    length = queries_all.shape[1]
    first_place = own_places[0]
    carry_start = (jnp.zeros(own_keys.shape, jnp.float32), jnp.zeros(own_values.shape, jnp.float32))

    def query_advance(carried, block_index):
        query_start = block_index * KEY_BLOCK

        def query_compute(inner):
            key_grads, value_grads = inner
            queries = split_heads(
                lax.dynamic_slice_in_dim(queries_all, query_start, KEY_BLOCK, 1).astype(
                    jnp.bfloat16
                )
            )
            head_grads = split_heads(
                lax.dynamic_slice_in_dim(grads_all, query_start, KEY_BLOCK, 1).astype(jnp.bfloat16)
            )
            total_block = jnp.transpose(
                lax.dynamic_slice_in_dim(totals_all, query_start, KEY_BLOCK, 1), (0, 2, 1)
            )
            delta_block = jnp.transpose(
                lax.dynamic_slice_in_dim(deltas_all, query_start, KEY_BLOCK, 1), (0, 2, 1)
            )
            query_segments = lax.dynamic_slice_in_dim(segments_all, query_start, KEY_BLOCK, 1)
            query_places = query_start + jnp.arange(KEY_BLOCK)
            allowed = allowed_mask(query_places, query_segments, own_places, own_segments)
            shares = jnp.where(
                allowed, jnp.exp(block_scores(queries, own_keys) - total_block[..., None]), 0.0
            )
            share_grads = jnp.einsum(
                "rqhd,rkhd->rhqk", head_grads, own_values, preferred_element_type=jnp.float32
            )
            score_grads = (shares * (share_grads - delta_block[..., None])).astype(jnp.bfloat16)
            key_grads = key_grads + jnp.einsum(
                "rhqk,rqhd->rkhd", score_grads, queries, preferred_element_type=jnp.float32
            )
            value_grads = value_grads + jnp.einsum(
                "rhqk,rqhd->rkhd",
                shares.astype(jnp.bfloat16),
                head_grads,
                preferred_element_type=jnp.float32,
            )
            return (key_grads, value_grads)

        return (
            lax.cond(query_start + KEY_BLOCK - 1 >= first_place, query_compute, unchanged, carried),
            None,
        )

    finished, unused = lax.scan(query_advance, carry_start, jnp.arange(length // KEY_BLOCK))
    return finished


def project_inputs(inputs, layer_weights, cosine, sine, rows_here):
    qkv_rows = layer_weights[0]
    norm_rows = layer_weights[4]
    gain_row = norm_rows[0].astype(jnp.float32)
    shift_row = norm_rows[1].astype(jnp.float32)
    normed, norm_pull = jax.vjp(layer_norm, inputs, gain_row, shift_row)
    normed_low = normed.astype(jnp.bfloat16)
    mixed = jnp.dot(
        normed_low, qkv_rows.reshape(qkv_rows.shape[0], -1), preferred_element_type=jnp.float32
    )
    mixed = mixed.reshape(rows_here, -1, 3, qkv_rows.shape[-1])
    queries = rotate(mixed[:, :, 0], cosine, sine).astype(jnp.bfloat16)
    key_rows = rotate(mixed[:, :, 1], cosine, sine).astype(jnp.bfloat16)
    value_rows = mixed[:, :, 2].astype(jnp.bfloat16)
    return (normed_low, norm_pull, queries, key_rows, value_rows)


def layer_forward(inputs, layer_weights, cosine, sine, segments, query_places):
    qkv_rows, out_rows, in_rows, down_rows, norm_rows = layer_weights
    rows_here, span_len = segments.shape
    normed_low, unused_pull, queries, key_rows, value_rows = project_inputs(
        inputs, layer_weights, cosine, sine, rows_here
    )
    keys_all, values_all, segments_all = (
        lax.all_gather(key_rows, "seq", axis=1, tiled=True),
        lax.all_gather(value_rows, "seq", axis=1, tiled=True),
        lax.all_gather(segments, "seq", axis=1, tiled=True),
    )
    head_queries = split_heads(queries)
    head_keys = split_heads(keys_all)
    head_values = split_heads(values_all)
    heads_here = head_queries.shape[2]
    totals_start = (
        jnp.full((rows_here, heads_here, span_len), low_score, jnp.float32),
        jnp.zeros((rows_here, heads_here, span_len), jnp.float32),
    )
    maxima, totals = key_sweep(
        total_step(head_queries),
        totals_start,
        head_keys,
        head_values,
        segments_all,
        query_places,
        segments,
    )
    log_totals = maxima + jnp.log(totals)
    outputs = key_sweep(
        value_step(head_queries, log_totals),
        jnp.zeros(head_queries.shape, jnp.float32),
        head_keys,
        head_values,
        segments_all,
        query_places,
        segments,
    )
    out_low = outputs.reshape(rows_here * span_len, -1).astype(jnp.bfloat16)
    attend_part = lax.dot_general(
        out_low, out_rows, (((1,), (1,)), ((), ())), preferred_element_type=jnp.float32
    )
    hidden = jnp.dot(normed_low, in_rows, preferred_element_type=jnp.float32)
    active_low = gelu_tanh(hidden).astype(jnp.bfloat16)
    feed_part = lax.dot_general(
        active_low, down_rows, (((1,), (1,)), ((), ())), preferred_element_type=jnp.float32
    )
    branch = lax.psum(attend_part + feed_part, "tp")
    return (inputs + branch + norm_rows[2].astype(jnp.float32), log_totals)


def layer_backward(
    inputs, out_grads, log_totals, layer_weights, cosine, sine, segments, query_places
):
    qkv_rows, out_rows, in_rows, down_rows, norm_rows = layer_weights
    rows_here, span_len = segments.shape
    token_count = rows_here * span_len
    normed_low, norm_pull, queries, key_rows, value_rows = project_inputs(
        inputs, layer_weights, cosine, sine, rows_here
    )
    keys_all, values_all, segments_all = (
        lax.all_gather(key_rows, "seq", axis=1, tiled=True),
        lax.all_gather(value_rows, "seq", axis=1, tiled=True),
        lax.all_gather(segments, "seq", axis=1, tiled=True),
    )
    head_queries = split_heads(queries)
    head_keys = split_heads(keys_all)
    head_values = split_heads(values_all)
    heads_here = head_queries.shape[2]
    grads_low = out_grads.astype(jnp.bfloat16)
    attend_grads = jnp.dot(grads_low, out_rows, preferred_element_type=jnp.float32).astype(
        jnp.bfloat16
    )
    attend_grads = attend_grads.reshape(rows_here, span_len, -1)
    head_grads = split_heads(attend_grads)
    revisit_start = (
        jnp.zeros(head_queries.shape, jnp.float32),
        jnp.zeros((rows_here, heads_here, span_len), jnp.float32),
    )
    outputs, deltas = key_sweep(
        revisit_step(head_queries, log_totals, head_grads),
        revisit_start,
        head_keys,
        head_values,
        segments_all,
        query_places,
        segments,
    )
    out_low = outputs.reshape(token_count, -1).astype(jnp.bfloat16)
    contract_tokens = (((0,), (0,)), ((), ()))
    contract_columns = (((1,), (1,)), ((), ()))
    out_weight_grads = lax.dot_general(
        grads_low, out_low, contract_tokens, preferred_element_type=jnp.float32
    )
    hidden = jnp.dot(normed_low, in_rows, preferred_element_type=jnp.float32)
    active, gelu_pull = jax.vjp(gelu_tanh, hidden)
    active_low = active.astype(jnp.bfloat16)
    active_grads = jnp.dot(grads_low, down_rows, preferred_element_type=jnp.float32)
    hidden_low = gelu_pull(active_grads)[0].astype(jnp.bfloat16)
    down_grads = lax.dot_general(
        grads_low, active_low, contract_tokens, preferred_element_type=jnp.float32
    )
    in_grads = lax.dot_general(
        normed_low, hidden_low, contract_tokens, preferred_element_type=jnp.float32
    )
    normed_grads = lax.dot_general(
        hidden_low, in_rows, contract_columns, preferred_element_type=jnp.float32
    )
    (query_grads,) = key_sweep(
        gradient_step(head_queries, log_totals, head_grads, deltas),
        (jnp.zeros(head_queries.shape, jnp.float32),),
        head_keys,
        head_values,
        segments_all,
        query_places,
        segments,
    )
    gathered = (
        lax.all_gather(queries.astype(jnp.float32), "seq", axis=1, tiled=True),
        lax.all_gather(attend_grads.astype(jnp.float32), "seq", axis=1, tiled=True),
        lax.all_gather(jnp.transpose(log_totals, (0, 2, 1)), "seq", axis=1, tiled=True),
        lax.all_gather(jnp.transpose(deltas, (0, 2, 1)), "seq", axis=1, tiled=True),
    )
    key_heads, value_heads = query_sweep(
        split_heads(key_rows),
        split_heads(value_rows),
        segments,
        query_places,
        gathered,
        segments_all,
    )
    key_grads = key_heads.reshape(rows_here, span_len, -1)
    value_grads = value_heads.reshape(rows_here, span_len, -1)
    score_scale = HEAD ** (-0.5)
    query_low = rotate_back(
        query_grads.reshape(rows_here, span_len, -1) * score_scale, cosine, sine
    ).astype(jnp.bfloat16)
    key_low = rotate_back(key_grads * score_scale, cosine, sine).astype(jnp.bfloat16)
    value_low = value_grads.astype(jnp.bfloat16)
    mixed_grads = jnp.stack([query_low, key_low, value_low], axis=2).reshape(token_count, -1)
    qkv_flat = qkv_rows.reshape(qkv_rows.shape[0], -1)
    qkv_grads = lax.dot_general(
        normed_low, mixed_grads, contract_tokens, preferred_element_type=jnp.float32
    )
    normed_grads = normed_grads + lax.dot_general(
        mixed_grads, qkv_flat, contract_columns, preferred_element_type=jnp.float32
    )
    normed_total = lax.psum(normed_grads, "tp")
    input_grads, gain_grads, shift_grads = norm_pull(normed_total)
    bias_grads = jnp.sum(out_grads, axis=0)
    small_grads = jnp.stack([gain_grads, shift_grads, bias_grads])
    return (
        out_grads + input_grads,
        (qkv_grads.reshape(qkv_rows.shape), out_weight_grads, in_grads, down_grads, small_grads),
    )


def adam_update(weight, first, second, gradient, factor_clip, rate, decay):
    clipped = gradient * factor_clip
    first_new = beta_one * first + (1.0 - beta_one) * clipped
    second_new = beta_two * second + (1.0 - beta_two) * clipped * clipped
    first_hat = first_new / (1.0 - beta_one**STEP)
    second_hat = second_new / (1.0 - beta_two**STEP)
    weight_new = weight - rate * (first_hat / (jnp.sqrt(second_hat) + adam_eps) + decay * weight)
    return (weight_new, first_new, second_new)


def shards(
    activations,
    cotangent,
    segment_ids,
    position_ids,
    qkv_weight,
    out_weight,
    in_weight,
    down_weight,
    norm_params,
    qkv_first,
    out_first,
    in_first,
    down_first,
    norm_first,
    qkv_second,
    out_second,
    in_second,
    down_second,
    norm_second,
):
    rows_here, span_len, model_width = activations.shape
    token_count = rows_here * span_len
    gathered = (
        lax.all_gather(qkv_weight.astype(jnp.bfloat16), "seq", axis=1, tiled=True),
        lax.all_gather(out_weight.astype(jnp.bfloat16), "seq", axis=1, tiled=True),
        lax.all_gather(in_weight.astype(jnp.bfloat16), "seq", axis=1, tiled=True),
        lax.all_gather(down_weight.astype(jnp.bfloat16), "seq", axis=1, tiled=True),
        lax.all_gather(norm_params.astype(jnp.bfloat16), "seq", axis=2, tiled=True),
    )
    local_width = gathered[0].shape[-1]
    cosine, sine = rotary_tables(position_ids, local_width)
    query_places = lax.axis_index("seq") * span_len + jnp.arange(span_len)
    layer_inputs = []
    kept_totals = []
    current = activations.reshape(token_count, model_width)
    for layer_index in range(LAYERS):
        layer_weights = tuple((piece_array[layer_index] for piece_array in gathered))
        layer_inputs.append(current)
        current, log_totals = layer_forward(
            current, layer_weights, cosine, sine, segment_ids, query_places
        )
        kept_totals.append(log_totals)
    result = current.reshape(activations.shape)
    grads_now = cotangent.reshape(token_count, model_width)
    collected = [None] * LAYERS
    for layer_index in reversed(range(LAYERS)):
        layer_weights = tuple((piece_array[layer_index] for piece_array in gathered))
        grads_now, layer_grads = layer_backward(
            layer_inputs[layer_index],
            grads_now,
            kept_totals[layer_index],
            layer_weights,
            cosine,
            sine,
            segment_ids,
            query_places,
        )
        collected[layer_index] = layer_grads
    stacked = tuple(
        (
            jnp.stack([collected[layer_index][kind_index] for layer_index in range(LAYERS)])
            for kind_index in range(5)
        )
    )
    reduced = (
        lax.psum_scatter(stacked[0], "seq", scatter_dimension=1, tiled=True),
        lax.psum_scatter(stacked[1], "seq", scatter_dimension=1, tiled=True),
        lax.psum_scatter(stacked[2], "seq", scatter_dimension=1, tiled=True),
        lax.psum_scatter(stacked[3], "seq", scatter_dimension=1, tiled=True),
        lax.psum_scatter(stacked[4], "seq", scatter_dimension=2, tiled=True),
    )
    matrix_squares = sum((jnp.sum(grad_block * grad_block) for grad_block in reduced[:4]))
    vector_squares = jnp.sum(reduced[4] * reduced[4]) / lax.axis_size("tp")
    total_squares = lax.psum(matrix_squares + vector_squares, ("seq", "tp"))
    grad_norm = jnp.sqrt(total_squares)
    factor_clip = jnp.minimum(1.0, clip_share * math.sqrt(NPARAM) / (grad_norm + 1e-06))
    qkv_new, qkv_first_new, qkv_second_new = adam_update(
        qkv_weight, qkv_first, qkv_second, reduced[0], factor_clip, rate_matrix, decay_matrix
    )
    out_new, out_first_new, out_second_new = adam_update(
        out_weight, out_first, out_second, reduced[1], factor_clip, rate_output, decay_matrix
    )
    in_new, in_first_new, in_second_new = adam_update(
        in_weight, in_first, in_second, reduced[2], factor_clip, rate_matrix, decay_matrix
    )
    down_new, down_first_new, down_second_new = adam_update(
        down_weight, down_first, down_second, reduced[3], factor_clip, rate_matrix, decay_matrix
    )
    norm_new, norm_first_new, norm_second_new = adam_update(
        norm_params, norm_first, norm_second, reduced[4], factor_clip, rate_vector, 0.0
    )
    bias_clipped = reduced[4][:, 2] * factor_clip
    return (
        result,
        grads_now.reshape(activations.shape),
        grad_norm,
        qkv_new,
        out_new,
        in_new,
        down_new,
        norm_new,
        qkv_first_new,
        out_first_new,
        in_first_new,
        down_first_new,
        norm_first_new,
        qkv_second_new,
        out_second_new,
        in_second_new,
        down_second_new,
        norm_second_new,
        bias_clipped,
    )


def solution(mesh):
    return jax.shard_map(
        shards,
        mesh=mesh,
        in_specs=(
            P(None, "seq", None),
            P(None, "seq", None),
            P(None, "seq"),
            P(None, "seq"),
            P(None, "seq", None, "tp"),
            P(None, "seq", "tp"),
            P(None, "seq", "tp"),
            P(None, "seq", "tp"),
            P(None, None, "seq"),
            P(None, "seq", None, "tp"),
            P(None, "seq", "tp"),
            P(None, "seq", "tp"),
            P(None, "seq", "tp"),
            P(None, None, "seq"),
            P(None, "seq", None, "tp"),
            P(None, "seq", "tp"),
            P(None, "seq", "tp"),
            P(None, "seq", "tp"),
            P(None, None, "seq"),
        ),
        out_specs=(
            P(None, "seq", None),
            P(None, "seq", None),
            P(),
            P(None, "seq", None, "tp"),
            P(None, "seq", "tp"),
            P(None, "seq", "tp"),
            P(None, "seq", "tp"),
            P(None, None, "seq"),
            P(None, "seq", None, "tp"),
            P(None, "seq", "tp"),
            P(None, "seq", "tp"),
            P(None, "seq", "tp"),
            P(None, None, "seq"),
            P(None, "seq", None, "tp"),
            P(None, "seq", "tp"),
            P(None, "seq", "tp"),
            P(None, "seq", "tp"),
            P(None, None, "seq"),
            P(None, "seq"),
        ),
        check_vma=False,
    )
```

profile of v0, /device:TPU:0, one launch (start us, length us, event | category | flops | bytes accessed | tf_op | source)
XLA Modules:
  0.0 2371.0 jit_solution(13650386179192367881)
XLA Ops:
  12.5 47.5 %all_gather.61 = bf16[2,3,1024]{1,0,2:T(2,128)(2,1)S(1)} all-gather(bf16[2,3,64]{1,0,2:T(2,128)(2,1)S(1)} %copy.362), channel_id=1, replica_groups=mesh['seq'=16,'tp'=2] {'seq'}, dimensions={2}, use_global_device_ids=true | all-gather | bytes 13056 | tf_op jit(solution)/shard_map/all_gather | solution.py:443
  60.9 16.8 fusion.174
  77.9 33.0 %all-gather.16.cloned.1.call-done = bf16[2,1024,3,512]{3,0,2,1:T(2,128)(2,1)} async-done(((bf16[2,64,3,512]{3,0,2,1:T(2,128)(2,1)}), bf16[2,1024,3,512]{3,0,2,1:T(2,128)(2,1)}) %all-gather.16.cloned.1.call-update) | async-done | bytes 6291472 | tf_op jit(solution)/shard_map/all_gather | solution.py:439
  151.4 38.3 %all-gather.2 = s32[16,64,2]{1,2,0:T(2,128)S(1)} all-gather(s32[1,64,2]{1,2,0:T(2,128)S(1)} %bitcast.501), channel_id=1, replica_groups=mesh['seq'=16,'tp'=2] {'seq'}, dimensions={0}, use_global_device_ids=true | all-gather | bytes 8704 | tf_op jit(solution)/shard_map/all_gather | solution.py:257
  215.0 52.9 %all-gather.36.cloned.1.call-done = bf16[2,1024,1,512]{3,1,2,0:T(8,128)(2,1)} async-done(((bf16[2,64,1,512]{3,1,2,0:T(8,128)(2,1)}), bf16[2,1024,1,512]{3,1,2,0:T(8,128)(2,1)}) %all-gather.36.cloned.1.call-update) | async-done | bytes 2097168 | tf_op jit(solution)/shard_map/all_gather | solution.py:256
  281.8 100.7 %all-gather.22.cloned.1.call-done = bf16[2,1024,2048]{2,1,0:T(8,128)(2,1)} async-done(((bf16[2,64,2048]{2,1,0:T(8,128)(2,1)}), bf16[2,1024,2048]{2,1,0:T(8,128)(2,1)}) %all-gather.22.cloned.1.call-update) | async-done | bytes 8388624 | tf_op jit(solution)/shard_map/all_gather | solution.py:441
  386.4 110.2 %all-gather.24.cloned.1.call-done = bf16[2,1024,2048]{2,1,0:T(8,128)(2,1)} async-done(((bf16[2,64,2048]{2,1,0:T(8,128)(2,1)}), bf16[2,1024,2048]{2,1,0:T(8,128)(2,1)}) %all-gather.24.cloned.1.call-update) | async-done | bytes 8388624 | tf_op jit(solution)/shard_map/all_gather | solution.py:442
  500.7 58.0 %all-gather.20.cloned.1.call-done = bf16[2,1024,512]{2,1,0:T(8,128)(2,1)} async-done(((bf16[2,64,512]{2,1,0:T(8,128)(2,1)}), bf16[2,1024,512]{2,1,0:T(8,128)(2,1)}) %all-gather.20.cloned.1.call-update) | async-done | bytes 2097168 | tf_op jit(solution)/shard_map/all_gather | solution.py:440
  597.9 46.7 %all-gather.30.cloned.1.call-done = bf16[2,1024,512]{2,0,1:T(2,128)(2,1)} async-done(((bf16[2,64,512]{2,0,1:T(2,128)(2,1)}), bf16[2,1024,512]{2,0,1:T(2,128)(2,1)}) %all-gather.30.cloned.1.call-update) | async-done | bytes 2097168 | tf_op jit(solution)/shard_map/all_gather | solution.py:367
  670.9 36.2 %all-gather.26.cloned.1.call-done = bf16[2,1024,512]{2,1,0:T(8,128)(2,1)} async-done(((bf16[2,64,512]{2,1,0:T(8,128)(2,1)}), bf16[2,1024,512]{2,1,0:T(8,128)(2,1)}) %all-gather.26.cloned.1.call-update) | async-done | bytes 2097168 | tf_op jit(solution)/shard_map/all_gather | solution.py:255
  716.3 53.7 %all-gather.38.cloned.1.call-done = bf16[2,1024,1,512]{3,1,2,0:T(8,128)(2,1)} async-done(((bf16[2,64,1,512]{3,1,2,0:T(8,128)(2,1)}), bf16[2,1024,1,512]{3,1,2,0:T(8,128)(2,1)}) %all-gather.38.cloned.1.call-update) | async-done | bytes 2097168 | tf_op jit(solution)/shard_map/all_gather | solution.py:256
  781.0 51.5 %all_gather.74 = f32[2,1024,8]{2,0,1:T(2,128)} all-gather(f32[2,64,8]{2,0,1:T(2,128)S(1)} %bitcast.523), channel_id=1, replica_groups=mesh['seq'=16,'tp'=2] {'seq'}, dimensions={1}, use_global_device_ids=true | all-gather | bytes 69632 | tf_op jit(solution)/shard_map/all_gather | solution.py:369
  833.8 45.2 %all_gather.72 = f32[2,1024,8]{2,0,1:T(2,128)} all-gather(f32[2,64,8]{2,0,1:T(2,128)} %bitcast.518), channel_id=1, replica_groups=mesh['seq'=16,'tp'=2] {'seq'}, dimensions={1}, use_global_device_ids=true | all-gather | bytes 69632 | tf_op jit(solution)/shard_map/all_gather | solution.py:368
  900.3 23.2 while.148
  948.4 15.2 all-reduce.7.cloned.1.call-done
  972.5 52.1 %all_gather.76 = f32[2,1024,8]{2,0,1:T(2,128)S(1)} all-gather(f32[2,64,8]{2,0,1:T(2,128)S(1)} %bitcast.517), channel_id=1, replica_groups=mesh['seq'=16,'tp'=2] {'seq'}, dimensions={1}, use_global_device_ids=true | all-gather | bytes 69632 | tf_op jit(solution)/shard_map/all_gather | solution.py:368
  1060.3 55.9 %all_gather.78 = f32[2,1024,8]{2,0,1:T(2,128)} all-gather(f32[2,64,8]{2,0,1:T(2,128)S(1)} %bitcast.524), channel_id=1, replica_groups=mesh['seq'=16,'tp'=2] {'seq'}, dimensions={1}, use_global_device_ids=true | all-gather | bytes 69632 | tf_op jit(solution)/shard_map/all_gather | solution.py:369
  1149.1 24.4 %while.151 = (s32[]{:T(128)}, f32[2,64,8,64]{1,3,2,0:T(8,128)}, f32[2,64,8,64]{1,3,2,0:T(8,128)}, s32[2]{0:T(128)}, s32[]{:T(128)}, /*index=5*/bf16[2,1024,512]{...) while((s32[]{:T(128)}, f32[2,64,8,64]{1,3,2,0:T(8,128)}, ...), condition=%wide.region_54.55_spmd.clone, body=%wide.region_51.54_spmd.clone.sunk | while | flops 272400960 | bytes 20596656 | solution.py:227
  1263.7 31.5 %reduce-scatter.16.cloned.1.call-done = f32[64,6]{1,0:T(8,128)} async-done(((f32[1024,6]{1,0:T(8,128)}), f32[64,6]{1,0:T(8,128)}) %reduce-scatter.16.cloned.1.call-update) | async-done | bytes 1552
  1297.4 91.4 %reduce-scatter.10.cloned.1.call-done = f32[2,64,512]{2,1,0:T(8,128)} async-done(((f32[2,1024,512]{2,1,0:T(8,128)}), f32[2,64,512]{2,1,0:T(8,128)}) %reduce-scatter.10.cloned.1.call-update) | async-done | bytes 262160 | tf_op jit(solution)/shard_map/reduce_scatter | solution.py:482
  1390.4 208.1 %reduce-scatter.8.cloned.1.call-done = f32[2,64,3,512]{3,1,2,0:T(8,128)} async-done(((f32[2,1024,3,512]{3,1,2,0:T(8,128)}), f32[2,64,3,512]{3,1,2,0:T(8,128)}) %reduce-scatter.8.cloned.1.call-update) | async-done | bytes 786448 | tf_op jit(solution)/shard_map/reduce_scatter | solution.py:481
  1601.8 345.2 %reduce-scatter.14.cloned.1.call-done = f32[2,64,2048]{2,1,0:T(8,128)} async-done(((f32[2,1024,2048]{2,1,0:T(8,128)}), f32[2,64,2048]{2,1,0:T(8,128)}) %reduce-scatter.14.cloned.1.call-update) | async-done | bytes 1048592 | tf_op jit(solution)/shard_map/reduce_scatter | solution.py:484
  1949.1 352.1 %reduce-scatter.12.cloned.1.call-done = f32[2,64,2048]{2,1,0:T(8,128)} async-done(((f32[2,1024,2048]{2,1,0:T(8,128)}), f32[2,64,2048]{2,1,0:T(8,128)}) %reduce-scatter.12.cloned.1.call-update) | async-done | bytes 1048592 | tf_op jit(solution)/shard_map/reduce_scatter | solution.py:483
  2305.5 44.4 %psum.39 = f32[]{:T(128)} all-reduce(f32[]{:T(128)S(6)} %add.705), channel_id=1, replica_groups=mesh['seq'=16,'tp'=2] {'seq','tp'}, use_global_device_ids=true, to_apply=%region_74.75 | all-reduce | flops 1 | bytes 8 | tf_op jit(solution)/shard_map/psum | solution.py:489
  (688 shorter events, 561.9 us)
Async XLA Ops:
  7.2 103.7 %all-gather.16.cloned.1.call-start = ((), (), s32[]{:S(2)}) async-start(), calls=%async_computation.5 | async-start | bytes 6684672 | tf_op jit(solution)/shard_map/all_gather | solution.py:439
  9.8 196.1 %all-gather.18.cloned.1.call-start = ((), (), s32[]{:S(2)}) async-start(), calls=%async_computation.6 | async-start | bytes 2228224 | tf_op jit(solution)/shard_map/all_gather | solution.py:255
  146.7 121.3 %all-gather.36.cloned.1.call-start = ((), (), s32[]{:S(2)}) async-start(), calls=%async_computation.21 | async-start | bytes 2228224 | tf_op jit(solution)/shard_map/all_gather | solution.py:256
  147.5 235.0 %all-gather.22.cloned.1.call-start = ((), (), s32[]{:S(2)}) async-start(), calls=%async_computation.8 | async-start | bytes 8912896 | tf_op jit(solution)/shard_map/all_gather | solution.py:441
  149.7 347.0 %all-gather.24.cloned.1.call-start = ((), (), s32[]{:S(2)}) async-start(), calls=%async_computation.9 | async-start | bytes 8912896 | tf_op jit(solution)/shard_map/all_gather | solution.py:442
  150.6 408.1 %all-gather.20.cloned.1.call-start = ((), (), s32[]{:S(2)}) async-start(), calls=%async_computation.7 | async-start | bytes 2228224 | tf_op jit(solution)/shard_map/all_gather | solution.py:440
  151.4 427.6 %all-reduce.5.cloned.1.call-start = ((), (), s32[]{:S(2)}) async-start(), calls=%async_computation.10 | async-start | bytes 1048576 | tf_op jit(solution)/shard_map/psum | solution.py:295
  561.4 83.2 %all-gather.30.cloned.1.call-start = ((), (), s32[]{:S(2)}) async-start(), calls=%async_computation.13 | async-start | bytes 2228224 | tf_op jit(solution)/shard_map/all_gather | solution.py:367
  564.0 143.1 %all-gather.26.cloned.1.call-start = ((), (), s32[]{:S(2)}) async-start(), calls=%async_computation.11 | async-start | bytes 2228224 | tf_op jit(solution)/shard_map/all_gather | solution.py:255
  592.3 177.7 %all-gather.38.cloned.1.call-start = ((), (), s32[]{:S(2)}) async-start(), calls=%async_computation.22 | async-start | bytes 2228224 | tf_op jit(solution)/shard_map/all_gather | solution.py:256
  593.0 301.7 %all-gather.28.cloned.1.call-start = ((), (), s32[]{:S(2)}) async-start(), calls=%async_computation.12 | async-start | bytes 2228224 | tf_op jit(solution)/shard_map/all_gather | solution.py:366
  593.8 369.9 %all-reduce.7.cloned.1.call-start = ((), (), s32[]{:S(2)}) async-start(), calls=%async_computation.14 | async-start | bytes 1048576 | tf_op jit(solution)/shard_map/psum | solution.py:395
  947.6 84.7 %all-gather.32.cloned.1.call-start = ((), (), s32[]{:S(2)}) async-start(), calls=%async_computation.15 | async-start | bytes 2228224 | tf_op jit(solution)/shard_map/all_gather | solution.py:366
  948.4 192.3 %all-gather.34.cloned.1.call-start = ((), (), s32[]{:S(2)}) async-start(), calls=%async_computation.16 | async-start | bytes 2228224 | tf_op jit(solution)/shard_map/all_gather | solution.py:367
  971.5 241.8 %all-reduce.9.cloned.1.call-start = ((), (), s32[]{:S(2)}) async-start(), calls=%async_computation.24 | async-start | bytes 2097152 | tf_op jit(solution)/shard_map/psum | solution.py:295
  1197.5 97.6 %reduce-scatter.16.cloned.1.call-start = ((), (), s32[]{:S(2)}) async-start(), calls=%async_computation.23 | async-start | bytes 557056
  1217.3 171.5 %reduce-scatter.10.cloned.1.call-start = ((), (), s32[]{:S(2)}) async-start(), calls=%async_computation.18 | async-start | bytes 4456448 | tf_op jit(solution)/shard_map/reduce_scatter | solution.py:482
  1221.3 377.2 %reduce-scatter.8.cloned.1.call-start = ((), (), s32[]{:S(2)}) async-start(), calls=%async_computation.17 | async-start | bytes 13369344 | tf_op jit(solution)/shard_map/reduce_scatter | solution.py:481
  1241.6 705.3 %reduce-scatter.14.cloned.1.call-start = ((), (), s32[]{:S(2)}) async-start(), calls=%async_computation.20 | async-start | bytes 17825792 | tf_op jit(solution)/shard_map/reduce_scatter | solution.py:484
  1251.6 1049.6 %reduce-scatter.12.cloned.1.call-start = ((), (), s32[]{:S(2)}) async-start(), calls=%async_computation.19 | async-start | bytes 17825792 | tf_op jit(solution)/shard_map/reduce_scatter | solution.py:483
  1262.8 1041.8 %copy-start.39 = (f32[128,1024]{1,0:T(8,128)S(1)}, f32[128,1024]{1,0:T(8,128)}, u32[]{:S(2)}) copy-start(f32[128,1024]{1,0:T(8,128)} %copy-done.38) | copy-start | bytes 1572868
  1390.4 960.9 %copy-start.116 = (f32[2,3,64]{2,0,1:T(2,128)S(1)}, f32[2,3,64]{2,0,1:T(2,128)}, u32[]{:S(2)}) copy-start(f32[2,3,64]{2,0,1:T(2,128)} %param.72) | copy-start | bytes 4612
  1390.4 960.9 %copy-start.117 = (f32[2,3,64]{2,0,1:T(2,128)S(1)}, f32[2,3,64]{2,0,1:T(2,128)}, u32[]{:S(2)}) copy-start(f32[2,3,64]{2,0,1:T(2,128)} %param.77) | copy-start | bytes 4612
  1390.4 962.6 %copy-start.43 = (f32[2,64,2048]{2,1,0:T(8,128)S(1)}, f32[2,64,2048]{2,1,0:T(8,128)}, u32[]{:S(2)}) copy-start(f32[2,64,2048]{2,1,0:T(8,128)} %param.66) | copy-start | bytes 3145732
  (122 other events, 4202.9 us)
Sparse Core Ops, SparseCore 0:
  11.4 99.4 all-gather.15
  146.8 59.0 all-gather.17
  208.7 59.2 all-gather.35
  271.2 111.2 all-gather.21
  385.7 110.9 all-gather.23
  499.8 58.8 all-gather.19
  561.6 17.2 all-reduce.4
  582.7 61.9 all-gather.29
  647.8 59.3 all-gather.25
  710.7 59.2 all-gather.37
  773.1 66.3 all-gather.27
  947.8 15.8 all-reduce.6
  966.4 65.8 all-gather.31
  1035.5 65.1 all-gather.33
  1197.7 15.5 all-reduce.8
  1217.4 77.7 reduce-scatter.15
  1297.3 91.4 reduce-scatter.9
  1394.3 204.1 reduce-scatter.7
  1600.9 345.9 reduce-scatter.13
  1949.2 352.0 reduce-scatter.11
where the time goes:
time: 2380 us; the launch traced here: 2370 us
  waiting for transfers between devices  1570 us (66%)
  blocking collectives  335 us (14%)
  local copies, waits for them, and re-layouts  181 us (8%)
  other arithmetic  131 us (6%)
  matrix products  106 us (4%)
  loops' own time  27.7 us (1%)
    reduce_scatter x1, waiting for transfers between devices, shards(): lax.psum_scatter(stacked[2], 'seq', scatter_dimension=1, tiled=True)  352 us
    reduce_scatter x1, waiting for transfers between devices, shards(): lax.psum_scatter(stacked[3], 'seq', scatter_dimension=1, tiled=True)  345 us
    reduce_scatter x1, waiting for transfers between devices, shards(): lax.psum_scatter(stacked[0], 'seq', scatter_dimension=1, tiled=True)  208 us
    all_gather x1, waiting for transfers between devices, shards(): lax.all_gather(down_weight.astype(jnp.bfloat16), 'seq', axis=1, tiled=True)  110 us
    all_gather x2, blocking collectives, layer_backward(): lax.all_gather(jnp.transpose(deltas, (0, 2, 1)), 'seq', axis=1, tiled=True)  107 us
    all_gather x2, waiting for transfers between devices, layer_forward(): lax.all_gather(value_rows, 'seq', axis=1, tiled=True)  107 us
    all_gather x1, waiting for transfers between devices, shards(): lax.all_gather(in_weight.astype(jnp.bfloat16), 'seq', axis=1, tiled=True)  101 us
    all_gather x2, blocking collectives, layer_backward(): lax.all_gather(jnp.transpose(log_totals, (0, 2, 1)), 'seq', axis=1, tiled...  97.3 us
  transfers between devices with their start and end apart: 20, of which 18 were waited for; matrix products, arithmetic and copies ran while one was open for 10% of the time, Pallas kernels for 0%

commit v1 on v0

v1 whole, which is shorter than its diff:
```python
import functools
import math

import jax
import jax.numpy as jnp
from jax import lax
from jax.experimental import pallas as pl
from jax.experimental.pallas import tpu as pltpu
from jax.sharding import PartitionSpec as P

HEAD = 64
ROTARY = 32
LAYERS = 2
STEP = 10
TILE = 256

norm_eps = 1e-05
beta_one = 0.9
beta_two = 0.999
adam_eps = 1e-08
rate_matrix = 0.05
rate_output = 0.15
rate_vector = 1.0
decay_matrix = 0.1
clip_share = 0.25
low_score = -1e30

MESH = pl.DeviceIdType.MESH
VM = pltpu.VMEM
DMA = pltpu.SemaphoreType.DMA
bf16 = jnp.bfloat16
f32 = jnp.float32
megabyte = 1 << 20


def split_sizes(members):
    nb = 1 << ((members.bit_length() - 1) // 2)
    return (members // nb, nb)


class Place:
    def __init__(self, n, rows):
        self.n, self.rows = n, rows
        self.members = n // rows
        self.na, self.nb = split_sizes(self.members)
        self.seq = lax.axis_index("seq")
        self.core = lax.axis_index("tp")
        self.row = lax.rem(self.seq, rows)
        self.member = self.seq // rows
        self.a = self.member // self.nb
        self.b = lax.rem(self.member, self.nb)

    def am(self, step):
        return lax.rem(self.a + step, self.na)

    def bm(self, step):
        return lax.rem(self.b + step, self.nb)

    def device(self, member, row=None, core=None):
        row = self.row if row is None else row
        return {"seq": member * self.rows + row, "tp": self.core if core is None else core}

    def at(self, a, b):
        return self.device(a * self.nb + b)

    def sibling(self):
        return self.device(self.member, core=1 - self.core)

    def partners(self):
        return [self.device(self.member, row=lax.rem(self.row + i, self.rows)) for i in range(1, self.rows)]

    def axis_peers(self):
        peers = [self.at(self.am(i), self.b) for i in range(1, self.na)]
        peers += [self.at(self.a, self.bm(j)) for j in range(1, self.nb)]
        return peers

    def other_members(self):
        return [self.device(lax.rem(self.member + i, self.members)) for i in range(1, self.members)]


def greet(devices):
    barrier = pltpu.get_barrier_semaphore()
    for device in devices:
        pl.semaphore_signal(barrier, inc=1, device_id=device, device_id_type=MESH)
    pl.semaphore_wait(barrier, len(devices))


class Sender:
    def __init__(self, send_sems):
        self.send_sems, self.copies = send_sems, []

    def send(self, src, dst, recv_sem, device):
        copy = pltpu.make_async_remote_copy(
            src_ref=src,
            dst_ref=dst,
            send_sem=self.send_sems.at[len(self.copies)],
            recv_sem=recv_sem,
            device_id=device,
            device_id_type=MESH,
        )
        copy.start()
        self.copies.append(copy)

    def arrived(self, dst, recv_sem, device):
        pltpu.make_async_remote_copy(
            src_ref=dst,
            dst_ref=dst,
            send_sem=self.send_sems.at[0],
            recv_sem=recv_sem,
            device_id=device,
            device_id_type=MESH,
        ).wait_recv()

    def finish(self):
        for copy in self.copies:
            copy.wait_send()


def remote_params(collective_id):
    return pltpu.CompilerParams(
        collective_id=collective_id, has_side_effects=True, vmem_limit_bytes=56 * megabyte
    )


def vmem_specs(count):
    return [pl.BlockSpec(memory_space=VM)] * count


def spread_kernel(n, rows, wide_ref, small_ref, pack_ref, chunk_ref, table_ref, weight_ref, *sems):
    (send_sems, chunk_sems, table_sems, block_sems, cross_sems, local_sems) = sems
    p = Place(n, rows)
    members = p.members
    everybody = [
        {"seq": lax.rem(p.seq + i, n), "tp": p.core} for i in range(1, n)
    ]
    greet(everybody)
    sender = Sender(send_sems)
    partners = [
        (lax.rem(p.row + i, rows), p.device(p.member, row=lax.rem(p.row + i, rows)))
        for i in range(1, rows)
    ]
    for device in everybody:
        sender.send(small_ref, table_ref.at[p.seq], table_sems.at[p.seq], device)
    for row, device in partners:
        sender.send(wide_ref.at[row], chunk_ref.at[p.row], chunk_sems.at[p.row], device)
    for layer in range(LAYERS):
        for i in range(1, members):
            member = lax.rem(p.member + i, members)
            sender.send(
                pack_ref.at[layer, member],
                weight_ref.at[layer, p.seq],
                block_sems.at[layer, p.member],
                p.device(member),
            )
        for row, device in partners:
            sender.send(
                pack_ref.at[layer, p.member],
                weight_ref.at[layer, p.seq],
                cross_sems.at[layer, p.seq],
                device,
            )
    own = [
        pltpu.make_async_copy(small_ref, table_ref.at[p.seq], local_sems.at[0]),
        pltpu.make_async_copy(wide_ref.at[p.row], chunk_ref.at[p.row], local_sems.at[1]),
    ]
    for layer in range(LAYERS):
        own.append(
            pltpu.make_async_copy(
                pack_ref.at[layer, p.member], weight_ref.at[layer, p.seq], local_sems.at[2 + layer]
            )
        )
    for copy in own:
        copy.start()
    for layer in range(LAYERS):
        for i in range(1, members):
            member = lax.rem(p.member + members - i, members)
            block = weight_ref.at[layer, member * rows + p.row]
            sender.arrived(block, block_sems.at[layer, member], p.sibling())
            for row, device in partners:
                sender.send(block, block, cross_sems.at[layer, member * rows + p.row], device)
    for i in range(1, n):
        seq = lax.rem(p.seq + i, n)
        sender.arrived(table_ref.at[seq], table_sems.at[seq], p.sibling())
    for row, device in partners:
        sender.arrived(chunk_ref.at[row], chunk_sems.at[row], p.sibling())
    for layer in range(LAYERS):
        for i in range(members):
            member = lax.rem(p.member + members - i, members)
            for row, device in partners:
                block = weight_ref.at[layer, member * rows + row]
                sender.arrived(block, cross_sems.at[layer, member * rows + row], p.sibling())
    sender.finish()
    for copy in own:
        copy.wait()


def spread(n, rows, wide, small, pack, collective_id):
    layers, members, height, columns = pack.shape
    sends = (n - 1) + (rows - 1) + layers * (members - 1 + members * (rows - 1))
    return pl.pallas_call(
        functools.partial(spread_kernel, n, rows),
        out_shape=(
            jax.ShapeDtypeStruct(wide.shape, wide.dtype),
            jax.ShapeDtypeStruct((n,) + small.shape, small.dtype),
            jax.ShapeDtypeStruct((layers, n, height, columns), pack.dtype),
        ),
        in_specs=vmem_specs(3),
        out_specs=tuple(vmem_specs(3)),
        scratch_shapes=[
            DMA((sends,)),
            DMA((rows,)),
            DMA((n,)),
            DMA((layers, members)),
            DMA((layers, n)),
            DMA((2 + layers,)),
        ],
        compiler_params=remote_params(collective_id),
        name="spread_inputs",
    )(wide, small, pack)


def gather_kernel(n, rows, count, x_ref, out_ref, *sems):
    send_sems, a_sems, b_sems, core_sems, local_sem = sems
    p = Place(n, rows)
    na, nb, core = p.na, p.nb, p.core
    sibling = p.sibling()
    greet(p.axis_peers() + [sibling])
    sender = Sender(send_sems)
    a_steps = [1, na - 1] + list(range(2, na - 1)) if na > 2 else [1]

    def slot(k, a, b):
        return out_ref.at[k, a * nb + b, core]

    for k in range(count):
        mine = x_ref.at[k, core]
        for i in a_steps:
            sender.send(mine, slot(k, p.a, p.b), a_sems.at[k, p.a], p.at(p.am(i), p.b))
        for j in range(1, nb):
            sender.send(mine, slot(k, p.a, p.b), b_sems.at[k, p.member], p.at(p.a, p.bm(j)))
    own = pltpu.make_async_copy(x_ref, out_ref.at[:, p.member], local_sem)
    own.start()
    for k in range(count):
        for i in a_steps:
            a = p.am(i)
            here = slot(k, a, p.b)
            sender.arrived(here, a_sems.at[k, a], sibling)
            for j in range(1, nb):
                sender.send(here, here, b_sems.at[k, a * nb + p.b], p.at(p.a, p.bm(j)))
            sender.send(here, here, core_sems.at[k, a * nb + p.b], sibling)
    for k in range(count):
        for i in [0] + a_steps:
            for j in range(1, nb):
                a, b = p.am(i), p.bm(j)
                here = slot(k, a, b)
                sender.arrived(here, b_sems.at[k, a * nb + b], sibling)
                sender.send(here, here, core_sems.at[k, a * nb + b], sibling)
    for k in range(count):
        for i in range(1, p.members):
            member = lax.rem(p.member + i, p.members)
            sender.arrived(out_ref.at[k, member, 1 - core], core_sems.at[k, member], sibling)
    sender.finish()
    own.wait()


def gather(n, rows, pieces, collective_id):
    stacked = jnp.stack(pieces)
    count, two, height, width = stacked.shape
    members = n // rows
    na, nb = split_sizes(members)
    sends = count * ((na - 1) * (nb + 1) + nb - 1 + na * (nb - 1))
    return pl.pallas_call(
        functools.partial(gather_kernel, n, rows, count),
        out_shape=jax.ShapeDtypeStruct((count, members, two, height, width), stacked.dtype),
        in_specs=vmem_specs(1),
        out_specs=vmem_specs(1)[0],
        scratch_shapes=[
            DMA((sends,)),
            DMA((count, na)),
            DMA((count, members)),
            DMA((count, members)),
            DMA,
        ],
        compiler_params=remote_params(collective_id),
        name="gather_tokens",
    )(stacked)


def reduce_kernel(n, rows, count, *refs):
    x_refs, (out_ref, core_buf, b_buf, a_buf, b_out, a_out) = refs[:count], refs[count : count + 6]
    send_sems, core_sems, b_sems, a_sems, out_sems = refs[count + 6 :]
    p = Place(n, rows)
    na, nb, core = p.na, p.nb, p.core
    sibling = p.sibling()
    greet(p.axis_peers() + [sibling])
    sender = Sender(send_sems)
    a_steps = list(range(2, na - 1)) + [1, na - 1, 0] if na > 2 else [1, 0]
    for k in range(count):
        for i in a_steps:
            for j in list(range(1, nb)) + [0]:
                m = p.am(i) * nb + p.bm(j)
                sender.send(x_refs[k].at[m, 1 - core], core_buf.at[k, m], core_sems.at[k, m], sibling)
    for k in range(count):
        for i in a_steps:
            for j in range(1, nb):
                a, b = p.am(i), p.bm(j)
                m = a * nb + b
                sender.arrived(core_buf.at[k, m], core_sems.at[k, m], sibling)
                b_out[k, m] = (x_refs[k][m, core].astype(f32) + core_buf[k, m].astype(f32)).astype(bf16)
                landing = a * nb + p.b
                sender.send(b_out.at[k, m], b_buf.at[k, landing], b_sems.at[k, landing], p.at(p.a, b))
    for k in range(count):
        for i in a_steps:
            a = p.am(i)
            m = a * nb + p.b
            sender.arrived(core_buf.at[k, m], core_sems.at[k, m], sibling)
            total = x_refs[k][m, core].astype(f32) + core_buf[k, m].astype(f32)
            for j in range(1, nb):
                q = a * nb + p.bm(j)
                sender.arrived(b_buf.at[k, q], b_sems.at[k, q], sibling)
                total = total + b_buf[k, q].astype(f32)
            if i:
                a_out[k, a] = total.astype(bf16)
                sender.send(a_out.at[k, a], a_buf.at[k, p.a], a_sems.at[k, p.a], p.at(a, p.b))
            else:
                out_ref[k, core] = total
    for k in range(count):
        for i in range(1, na):
            a = p.am(i)
            sender.arrived(a_buf.at[k, a], a_sems.at[k, a], sibling)
            out_ref[k, core] += a_buf[k, a].astype(f32)
        sender.send(out_ref.at[k, core], out_ref.at[k, core], out_sems.at[k], sibling)
    for k in range(count):
        sender.arrived(out_ref.at[k, 1 - core], out_sems.at[k], sibling)
    sender.finish()


def reduce(n, rows, pieces, collective_id):
    count = len(pieces)
    members, two, height, width = pieces[0].shape
    na, nb = split_sizes(members)
    sends = count * (members + na * (nb - 1) + na)
    return pl.pallas_call(
        functools.partial(reduce_kernel, n, rows, count),
        out_shape=jax.ShapeDtypeStruct((count, two, height, width), f32),
        in_specs=vmem_specs(count),
        out_specs=vmem_specs(1)[0],
        scratch_shapes=[
            VM((count, members, height, width), bf16),
            VM((count, members, height, width), bf16),
            VM((count, na, height, width), bf16),
            VM((count, members, height, width), bf16),
            VM((count, na, height, width), bf16),
            DMA((sends,)),
            DMA((count, members)),
            DMA((count, members)),
            DMA((count, na)),
            DMA((count,)),
        ],
        compiler_params=remote_params(collective_id),
        name="reduce_tokens",
    )(*pieces)


def collect_kernel(n, rows, *refs):
    (first_ref, second_ref, wide_ref, small_ref, grad_ref, back_ref, table_ref) = refs[:7]
    (cross_buf, block_out, send_sems, cross_sems, block_sems, back_sems, table_sems, local_sems) = refs[7:]
    grads = (first_ref, second_ref)
    p = Place(n, rows)
    members = p.members
    everybody = [{"seq": lax.rem(p.seq + i, n), "tp": p.core} for i in range(1, n)]
    greet(everybody)
    sender = Sender(send_sems)
    partners = [
        (lax.rem(p.row + i, rows), p.device(p.member, row=lax.rem(p.row + i, rows)))
        for i in range(1, rows)
    ]
    order = [lax.rem(p.member + i, members) for i in range(1, members)] + [p.member]
    for i in range(1, n):
        seq = lax.rem(p.seq + i, n)
        sender.send(small_ref.at[seq], table_ref.at[p.seq], table_sems.at[p.seq], {"seq": seq, "tp": p.core})
    for layer in range(LAYERS):
        for member in order:
            for row, device in partners:
                sender.send(
                    grads[layer].at[member * rows + row],
                    cross_buf.at[layer, p.row, member],
                    cross_sems.at[layer, p.row, member],
                    device,
                )
    for row, device in partners:
        sender.send(wide_ref.at[row], back_ref.at[p.row], back_sems.at[p.row], device)
    own = [
        pltpu.make_async_copy(small_ref.at[p.seq], table_ref.at[p.seq], local_sems.at[0]),
        pltpu.make_async_copy(wide_ref.at[p.row], back_ref.at[p.row], local_sems.at[1]),
    ]
    for copy in own:
        copy.start()
    for layer in range(LAYERS):
        for i in list(range(1, members)) + [0]:
            member = lax.rem(p.member + i, members)
            total = grads[layer][member * rows + p.row].astype(f32)
            for row, device in partners:
                buffer = cross_buf.at[layer, row, member]
                sender.arrived(buffer, cross_sems.at[layer, row, member], p.sibling())
                total = total + buffer[...].astype(f32)
            if i:
                block_out[layer, member] = total.astype(bf16)
                sender.send(
                    block_out.at[layer, member],
                    grad_ref.at[layer, p.member],
                    block_sems.at[layer, p.member],
                    p.device(member),
                )
            else:
                grad_ref[layer, member] = total.astype(bf16)
    for i in range(1, n):
        seq = lax.rem(p.seq + i, n)
        sender.arrived(table_ref.at[seq], table_sems.at[seq], p.sibling())
    for row, device in partners:
        sender.arrived(back_ref.at[row], back_sems.at[row], p.sibling())
    for layer in range(LAYERS):
        for i in range(1, members):
            member = lax.rem(p.member + members - i, members)
            sender.arrived(grad_ref.at[layer, member], block_sems.at[layer, member], p.sibling())
    sender.finish()
    for copy in own:
        copy.wait()


def collect(n, rows, first, second, wide, small, collective_id):
    unused, height, columns = first.shape
    members = n // rows
    sends = (n - 1) + (rows - 1) + LAYERS * (members * (rows - 1) + members - 1)
    return pl.pallas_call(
        functools.partial(collect_kernel, n, rows),
        out_shape=(
            jax.ShapeDtypeStruct((LAYERS, members, height, columns), bf16),
            jax.ShapeDtypeStruct(wide.shape, wide.dtype),
            jax.ShapeDtypeStruct(small.shape, small.dtype),
        ),
        in_specs=vmem_specs(4),
        out_specs=tuple(vmem_specs(3)),
        scratch_shapes=[
            VM((LAYERS, rows, members, height, columns), bf16),
            VM((LAYERS, members, height, columns), bf16),
            DMA((sends,)),
            DMA((LAYERS, rows, members)),
            DMA((LAYERS, members)),
            DMA((rows,)),
            DMA((n,)),
            DMA((2,)),
        ],
        compiler_params=remote_params(collective_id),
        name="collect_gradients",
    )(first, second, wide, small)


def share_kernel(n, x_ref, out_ref, send_sems, recv_sems, local_sem):
    seq, core = lax.axis_index("seq"), lax.axis_index("tp")
    others = []
    for i in range(n):
        for j in range(2):
            if i or j:
                others.append((lax.rem(seq + i, n), lax.rem(core + j, 2)))
    greet([{"seq": s, "tp": c} for s, c in others])
    sender = Sender(send_sems)
    here = seq * 2 + core
    for s, c in others:
        sender.send(x_ref, out_ref.at[here], recv_sems.at[here], {"seq": s, "tp": c})
    own = pltpu.make_async_copy(x_ref, out_ref.at[here], local_sem)
    own.start()
    for s, c in others:
        sender.arrived(out_ref.at[s * 2 + c], recv_sems.at[s * 2 + c], {"seq": s, "tp": c})
    sender.finish()
    own.wait()


def share(n, x, collective_id):
    return pl.pallas_call(
        functools.partial(share_kernel, n),
        out_shape=jax.ShapeDtypeStruct((2 * n,) + x.shape, x.dtype),
        in_specs=vmem_specs(1),
        out_specs=vmem_specs(1)[0],
        scratch_shapes=[DMA((2 * n,)), DMA((2 * n,)), DMA],
        compiler_params=remote_params(collective_id),
        name="share_squares",
    )(x)


def dot(left, right):
    return jnp.dot(left, right, preferred_element_type=f32)


def dot_nt(left, right):
    return lax.dot_general(left, right, (((1,), (1,)), ((), ())), preferred_element_type=f32)


def dot_tn(left, right):
    return lax.dot_general(left, right, (((0,), (0,)), ((), ())), preferred_element_type=f32)


def swap_lanes(values):
    width = values.shape[-1]
    lane = lax.broadcasted_iota(jnp.int32, values.shape, 1)
    after = pltpu.roll(values, width - 1, 1)
    before = pltpu.roll(values, 1, 1)
    return jnp.where(lane % 2 == 0, after, before)


gelu_scale = 0.7978845608
gelu_cubic = 0.044715


def gelu(z):
    return 0.5 * z * (1.0 + jnp.tanh(gelu_scale * (z + gelu_cubic * z * z * z)))


def gelu_slope(z):
    inner = jnp.tanh(gelu_scale * (z + gelu_cubic * z * z * z))
    slope = gelu_scale * (1.0 + 3.0 * gelu_cubic * z * z)
    return 0.5 * (1.0 + inner) + 0.5 * z * (1.0 - inner * inner) * slope


def query_tiles(length, share, rows):
    tile = max(64, min(TILE, TILE * 1024 // length))
    first = 0
    if share > 1:
        first = lax.rem(lax.axis_index("seq") // rows, share) * (length // share)
    for i in range(length // share // tile):
        start = pl.multiple_of(first + i * tile, tile) if share > 1 else i * tile
        yield pl.ds(start, tile), start, ((i + 1) * tile if share == 1 else length)


def visible(start, keys, seg_col, seg_row):
    tile = seg_col.shape[0]
    place = start + lax.broadcasted_iota(jnp.int32, (tile, keys), 0)
    other = lax.broadcasted_iota(jnp.int32, (tile, keys), 1)
    return (other <= place) & (seg_col == seg_row)


def forward_kernel(batch, share, ff, h_ref, w_ref, cos_ref, sin_ref, segc_ref, segr_ref, *outs):
    part_ref, q_ref, k_ref, v_ref, o_ref, lse_ref, a_ref, z_ref = outs
    length = h_ref.shape[0]
    f = 4 * HEAD

    @pl.loop(0, length // TILE)
    def project(t):
        rows = pl.ds(t * TILE, TILE)
        h = h_ref[rows, :]
        mixed = dot(h, w_ref[:, :f])
        qk = mixed[:, : 2 * HEAD]
        qk = qk * cos_ref[rows, :] + swap_lanes(qk) * sin_ref[rows, :]
        q_ref[rows, :] = (qk[:, :HEAD].astype(bf16).astype(f32) * HEAD**-0.5).astype(bf16)
        k_ref[rows, :] = qk[:, HEAD:].astype(bf16)
        v_ref[rows, :] = mixed[:, 2 * HEAD : 3 * HEAD].astype(bf16)
        z = dot(h, w_ref[:, f : f + ff])
        z_ref[rows, :] = z
        a_ref[rows, :] = gelu(z).astype(bf16)

    if share > 1:
        o_ref[...] = jnp.zeros_like(o_ref)
        lse_ref[...] = jnp.zeros_like(lse_ref)
    for rows, start, keys in query_tiles(length, share, batch):
        scores = dot_nt(q_ref[rows, :], k_ref[:keys, :])
        seen = visible(start, keys, segc_ref[rows, :], segr_ref[:, :keys])
        scores = jnp.where(seen, scores, low_score)
        peak = jnp.max(scores, axis=1, keepdims=True)
        weights = jnp.exp(scores - peak)
        total = jnp.sum(weights, axis=1, keepdims=True)
        lse_ref[rows, :] = peak + jnp.log(total)
        shares = (weights * (1.0 / total)).astype(bf16)
        o_ref[rows, :] = dot(shares, v_ref[:keys, :]).astype(bf16)

    @pl.loop(0, length // TILE)
    def branch(t):
        rows = pl.ds(t * TILE, TILE)
        out = dot_nt(o_ref[rows, :], w_ref[:, 3 * HEAD : f])
        out = out + dot_nt(a_ref[rows, :], w_ref[:, f + ff : f + 2 * ff])
        part_ref[rows, :] = out.astype(bf16)


def forward(batch, share, ff, h, w, cosine, sine, seg_col, seg_row):
    length, width = h.shape
    column = jax.ShapeDtypeStruct((length, HEAD), bf16)
    return pl.pallas_call(
        functools.partial(forward_kernel, batch, share, ff),
        out_shape=(
            jax.ShapeDtypeStruct((length, width), bf16),
            column,
            column,
            column,
            column,
            jax.ShapeDtypeStruct((length, 1), f32),
            jax.ShapeDtypeStruct((length, ff), bf16),
            jax.ShapeDtypeStruct((length, ff), f32),
        ),
        in_specs=vmem_specs(6),
        out_specs=tuple(vmem_specs(8)),
        compiler_params=pltpu.CompilerParams(vmem_limit_bytes=56 * megabyte),
        name="layer_forward",
    )(h, w, cosine, sine, seg_col, seg_row)


def backward_kernel(batch, share, ff, g_ref, h_ref, w_ref, cos_ref, sin_ref, segc_ref, segr_ref, *refs):
    q_ref, k_ref, v_ref, o_ref, lse_ref, a_ref, z_ref, part_ref, dw_ref = refs[:9]
    dz_ref, do_ref, dq_ref, dk_ref, dv_ref, mix_ref = refs[9:]
    length, width = h_ref.shape
    f = 4 * HEAD

    @pl.loop(0, length // TILE)
    def feed(t):
        rows = pl.ds(t * TILE, TILE)
        g = g_ref[rows, :]
        da = dot(g, w_ref[:, f + ff : f + 2 * ff])
        dz_ref[rows, :] = (da * gelu_slope(z_ref[rows, :])).astype(bf16)
        do_ref[rows, :] = dot(g, w_ref[:, :f])[:, 3 * HEAD :].astype(bf16)

    dk_ref[...] = jnp.zeros_like(dk_ref)
    dv_ref[...] = jnp.zeros_like(dv_ref)
    if share > 1:
        dq_ref[...] = jnp.zeros_like(dq_ref)
    for rows, start, keys in query_tiles(length, share, batch):
        q, head_grad = q_ref[rows, :], do_ref[rows, :]
        scores = dot_nt(q, k_ref[:keys, :])
        seen = visible(start, keys, segc_ref[rows, :], segr_ref[:, :keys])
        shares = jnp.where(seen, jnp.exp(scores - lse_ref[rows, :]), 0.0)
        share_grads = dot_nt(head_grad, v_ref[:keys, :])
        delta = jnp.sum(shares * share_grads, axis=1, keepdims=True)
        score_grads = (shares * (share_grads - delta)).astype(bf16)
        dq_ref[rows, :] = dot(score_grads, k_ref[:keys, :]) * HEAD**-0.5
        dk_ref[:keys, :] += dot_tn(score_grads, q)
        dv_ref[:keys, :] += dot_tn(shares.astype(bf16), head_grad)

    @pl.loop(0, length // TILE)
    def inward(t):
        rows = pl.ds(t * TILE, TILE)
        qk = jnp.concatenate([dq_ref[rows, :], dk_ref[rows, :]], axis=1)
        qk = qk * cos_ref[rows, :] + swap_lanes(qk * sin_ref[rows, :])
        rest = jnp.concatenate([dv_ref[rows, :], jnp.zeros((TILE, HEAD), f32)], axis=1)
        mix = jnp.concatenate([qk, rest], axis=1).astype(bf16)
        mix_ref[rows, :] = mix
        out = dot_nt(mix, w_ref[:, :f]) + dot_nt(dz_ref[rows, :], w_ref[:, f : f + ff])
        part_ref[rows, :] = out.astype(bf16)

    @pl.loop(0, width // TILE)
    def weights(t):
        rows = pl.ds(t * TILE, TILE)
        h, g = h_ref[:, rows], g_ref[:, rows]
        mixed = dot_tn(h, mix_ref[...])
        out = dot_tn(g, o_ref[...])
        dw_ref[rows, :f] = jnp.concatenate([mixed[:, : 3 * HEAD], out], axis=1).astype(bf16)
        dw_ref[rows, f : f + ff] = dot_tn(h, dz_ref[...]).astype(bf16)
        dw_ref[rows, f + ff : f + 2 * ff] = dot_tn(g, a_ref[...]).astype(bf16)


def backward(batch, share, ff, g, h, w, cosine, sine, seg_col, seg_row, kept):
    length, width = h.shape
    return pl.pallas_call(
        functools.partial(backward_kernel, batch, share, ff),
        out_shape=(
            jax.ShapeDtypeStruct((length, width), bf16),
            jax.ShapeDtypeStruct(w.shape, bf16),
        ),
        in_specs=vmem_specs(14),
        out_specs=tuple(vmem_specs(2)),
        scratch_shapes=[
            VM((length, ff), bf16),
            VM((length, HEAD), bf16),
            VM((length, HEAD), f32),
            VM((length, HEAD), f32),
            VM((length, HEAD), f32),
            VM((length, 4 * HEAD), bf16),
        ],
        compiler_params=pltpu.CompilerParams(vmem_limit_bytes=60 * megabyte),
        name="layer_backward",
    )(g, h, w, cosine, sine, seg_col, seg_row, *kept)


def layer_norm(inputs):
    average = jnp.mean(inputs, axis=-1, keepdims=True)
    centred = inputs - average
    spread_here = jnp.mean(centred * centred, axis=-1, keepdims=True)
    inverse = lax.rsqrt(spread_here + norm_eps)
    return (centred * inverse, inverse)


def norm_back(grads, normed_grads, xhat, inverse, gain):
    scaled = normed_grads * gain
    average = jnp.mean(scaled, axis=-1, keepdims=True)
    along = jnp.mean(scaled * xhat, axis=-1, keepdims=True)
    return grads + (scaled - average - xhat * along) * inverse


def rotary_tables(positions):
    column = jnp.arange(HEAD)
    inside = column < ROTARY
    pair_index = column % ROTARY // 2
    frequency = jnp.exp(pair_index.astype(f32) * (-2.0 * math.log(10000.0) / ROTARY))
    angles = positions[:, None] * frequency
    cosine = jnp.where(inside, jnp.cos(angles), 1.0)
    signed = jnp.where(column % 2 == 0, -1.0, 1.0)
    sine = jnp.where(inside, signed * jnp.sin(angles), 0.0)
    return (jnp.tile(cosine, (1, 2)), jnp.tile(sine, (1, 2)))


def pad_lanes(values, width=128):
    return jnp.pad(values, [(0, 0)] * (values.ndim - 1) + [(0, width - values.shape[-1])])


def adam_update(weight, first, second, gradient, factor_clip, rate, decay):
    clipped = gradient * factor_clip
    first_new = beta_one * first + (1.0 - beta_one) * clipped
    second_new = beta_two * second + (1.0 - beta_two) * clipped * clipped
    first_hat = first_new / (1.0 - beta_one**STEP)
    second_hat = second_new / (1.0 - beta_two**STEP)
    weight_new = weight - rate * (first_hat / (jnp.sqrt(second_hat) + adam_eps) + decay * weight)
    return (weight_new, first_new, second_new)


def pack_weights(n, rows, qkv_weight, out_weight, in_weight, down_weight):
    layers, height = qkv_weight.shape[:2]
    members = n // rows
    heads = qkv_weight.shape[3] // HEAD
    share = members // heads
    ff = in_weight.shape[2] // members
    mixed = jnp.concatenate([qkv_weight, out_weight[:, :, None, :]], axis=2).astype(bf16)
    mixed = mixed.reshape(layers, height, 4, heads, HEAD).transpose(0, 3, 1, 2, 4)
    mixed = mixed.reshape(layers, heads, height, 4 * HEAD)
    if share > 1:
        mixed = jnp.repeat(mixed, share, axis=1)
    feeds = [
        weight.astype(bf16).reshape(layers, height, members, ff).transpose(0, 2, 1, 3)
        for weight in (in_weight, down_weight)
    ]
    return jnp.concatenate([mixed] + feeds, axis=3)


def unpack_gradients(grads, heads, ff):
    layers, members, height, unused = grads.shape
    grads = grads.astype(f32)
    share = members // heads
    mixed = grads[..., : 4 * HEAD]
    if share > 1:
        mixed = mixed.reshape(layers, heads, share, height, 4 * HEAD).sum(2)
    mixed = mixed.reshape(layers, heads, height, 4, HEAD).transpose(0, 2, 3, 1, 4)
    mixed = mixed.reshape(layers, height, 4, heads * HEAD)
    feeds = [
        grads[..., 4 * HEAD + k * ff : 4 * HEAD + (k + 1) * ff]
        .transpose(0, 2, 1, 3)
        .reshape(layers, height, members * ff)
        for k in range(2)
    ]
    return (mixed[:, :, :3], mixed[:, :, 3], feeds[0], feeds[1])


def shards(
    n,
    activations,
    cotangent,
    segment_ids,
    position_ids,
    qkv_weight,
    out_weight,
    in_weight,
    down_weight,
    norm_params,
    qkv_first,
    out_first,
    in_first,
    down_first,
    norm_first,
    qkv_second,
    out_second,
    in_second,
    down_second,
    norm_second,
):
    rows, span, width = activations.shape
    members = n // rows
    length = n * span
    half = rows * span // 2
    heads = qkv_weight.shape[3] // HEAD
    share_queries = members // heads
    ff = in_weight.shape[2] // members
    row = lax.axis_index("seq") % rows

    pack = pack_weights(n, rows, qkv_weight, out_weight, in_weight, down_weight)
    norm_low = norm_params.astype(bf16).astype(f32).reshape(LAYERS * 3, -1)
    small = jnp.concatenate(
        [
            pad_lanes(norm_low),
            pad_lanes(position_ids.astype(f32)),
            pad_lanes(segment_ids.astype(f32)),
        ]
    )
    small = jnp.pad(small, ((0, -small.shape[0] % 8), (0, 0)))
    wide = jnp.stack([activations, cotangent], axis=1)
    chunk, table, weights = spread(n, rows, wide, small, pack, 0)
    weights = weights.reshape(LAYERS, width, -1)
    inputs = chunk[:, 0].reshape(rows * span, width)
    out_grads = chunk[:, 1].reshape(rows * span, width)
    own_columns = norm_params.shape[-1]
    norms = table[:, : LAYERS * 3, :own_columns].transpose(1, 0, 2).reshape(LAYERS, 3, width)
    positions = lax.dynamic_index_in_dim(table, LAYERS * 3 + row, 1, False)[:, :span].reshape(length)
    segments = lax.dynamic_index_in_dim(table, LAYERS * 3 + rows + row, 1, False)[:, :span].reshape(length)
    cosine, sine = rotary_tables(positions)
    places = (cosine, sine, segments[:, None], segments[None, :])

    def halves(values):
        return values.astype(bf16).reshape(2, half, width)

    def whole(values):
        return values.reshape(length, width)

    def parts(values):
        return values.reshape(members, 2, half, width)

    xhat_0, inverse_0 = layer_norm(inputs)
    normed = xhat_0 * norms[0, 0] + norms[0, 1]
    got = gather(n, rows, [halves(normed), halves(out_grads)], 1)
    normed_0, grads_1 = whole(got[0]), whole(got[1])
    part, *kept_0 = forward(rows, share_queries, ff, normed_0, weights[0], *places)
    branch = reduce(n, rows, [parts(part)], 2)[0].reshape(inputs.shape)
    middle = inputs + branch + norms[0, 2]
    xhat_1, inverse_1 = layer_norm(middle)
    normed = xhat_1 * norms[1, 0] + norms[1, 1]
    normed_1 = whole(gather(n, rows, [halves(normed)], 3)[0])
    part, *kept_1 = forward(rows, share_queries, ff, normed_1, weights[1], *places)
    back_part, weight_grads_1 = backward(rows, share_queries, ff, grads_1, normed_1, weights[1], *places, kept_1)
    sums = reduce(n, rows, [parts(part), parts(back_part)], 4).reshape((2,) + inputs.shape)
    result = middle + sums[0] + norms[1, 2]
    normed_grads_1 = sums[1]
    grads_mid = norm_back(out_grads, normed_grads_1, xhat_1, inverse_1, norms[1, 0])
    grads_0 = whole(gather(n, rows, [halves(grads_mid)], 5)[0])
    back_part, weight_grads_0 = backward(rows, share_queries, ff, grads_0, normed_0, weights[0], *places, kept_0)
    normed_grads_0 = reduce(n, rows, [parts(back_part)], 6)[0].reshape(inputs.shape)
    input_grad = norm_back(grads_mid, normed_grads_0, xhat_0, inverse_0, norms[0, 0])

    small_grads = jnp.stack(
        [
            jnp.sum(normed_grads_0 * xhat_0, axis=0),
            jnp.sum(normed_grads_0, axis=0),
            jnp.sum(grads_mid, axis=0),
            jnp.sum(normed_grads_1 * xhat_1, axis=0),
            jnp.sum(normed_grads_1, axis=0),
            jnp.sum(out_grads, axis=0),
        ]
    )
    small_grads = pad_lanes(small_grads.reshape(LAYERS * 3, n, own_columns).transpose(1, 0, 2))
    small_grads = jnp.pad(small_grads, ((0, 0), (0, 8 - LAYERS * 3), (0, 0)))
    wide_out = jnp.stack([result.reshape(rows, span, width), input_grad.reshape(rows, span, width)], axis=1)
    height = width // n
    grads, wide_back, table_back = collect(
        n,
        rows,
        weight_grads_0.reshape(n, height, -1),
        weight_grads_1.reshape(n, height, -1),
        wide_out,
        small_grads,
        7,
    )
    norm_grads = jnp.sum(table_back, axis=0)[: LAYERS * 3, :own_columns].reshape(norm_params.shape)
    qkv_grads, out_weight_grads, in_grads, down_grads = unpack_gradients(grads, heads, ff)
    matrix_squares = sum(
        (jnp.sum(block * block) for block in (qkv_grads, out_weight_grads, in_grads, down_grads))
    )
    squares = matrix_squares + jnp.sum(norm_grads * norm_grads) / 2
    everyone = share(n, jnp.full((8, 128), squares, f32), 8)
    grad_norm = jnp.sqrt(jnp.sum(everyone[:, 0, 0]))
    total_parameters = LAYERS * width * (4 * 2 * heads * HEAD + 2 * 2 * members * ff + 3)
    factor_clip = jnp.minimum(1.0, clip_share * math.sqrt(total_parameters) / (grad_norm + 1e-06))
    qkv_new, qkv_first_new, qkv_second_new = adam_update(
        qkv_weight, qkv_first, qkv_second, qkv_grads, factor_clip, rate_matrix, decay_matrix
    )
    out_new, out_first_new, out_second_new = adam_update(
        out_weight, out_first, out_second, out_weight_grads, factor_clip, rate_output, decay_matrix
    )
    in_new, in_first_new, in_second_new = adam_update(
        in_weight, in_first, in_second, in_grads, factor_clip, rate_matrix, decay_matrix
    )
    down_new, down_first_new, down_second_new = adam_update(
        down_weight, down_first, down_second, down_grads, factor_clip, rate_matrix, decay_matrix
    )
    norm_new, norm_first_new, norm_second_new = adam_update(
        norm_params, norm_first, norm_second, norm_grads, factor_clip, rate_vector, 0.0
    )
    bias_clipped = norm_grads[:, 2] * factor_clip
    return (
        wide_back[:, 0],
        wide_back[:, 1],
        grad_norm,
        qkv_new,
        out_new,
        in_new,
        down_new,
        norm_new,
        qkv_first_new,
        out_first_new,
        in_first_new,
        down_first_new,
        norm_first_new,
        qkv_second_new,
        out_second_new,
        in_second_new,
        down_second_new,
        norm_second_new,
        bias_clipped,
    )


def solution(mesh):
    tokens = P(None, "seq", None)
    qkv = P(None, "seq", None, "tp")
    matrix = P(None, "seq", "tp")
    norm = P(None, None, "seq")
    kinds = (qkv, matrix, matrix, matrix, norm)
    return jax.shard_map(
        functools.partial(shards, mesh.shape["seq"]),
        mesh=mesh,
        in_specs=(tokens, tokens, P(None, "seq"), P(None, "seq")) + kinds * 3,
        out_specs=(tokens, tokens, P()) + kinds * 3 + (P(None, "seq"),),
        check_vma=False,
    )
```

time: 2380 us -> 427 us (0.18)
  waiting for transfers between devices: 1570 us -> 0 us
  Pallas kernels: 0 us -> 345 us
  blocking collectives: 335 us -> 0 us
  local copies, waits for them, and re-layouts: 181 us -> 35.5 us
  matrix products: 106 us -> 0 us
  other arithmetic: 131 us -> 35.4 us
  loops' own time: 27.7 us -> 0 us
    reduce_scatter x4 -> x0, waiting for transfers between devices: 997 us -> none  [the longest x1 352 us: shards(): lax.psum_scatter(stacked[2], 'seq', scatter_dimension=1, tiled=True)]
    all_gather x12 -> x0, waiting for transfers between devices: 512 us -> none  [the longest x1 110 us: shards(): lax.all_gather(down_weight.astype(jnp.bfloat16), 'seq', axis=1, tiled=True)]
    pallas_call x0 -> x13, Pallas kernels: none -> 345 us  [the longest x3 89.1 us: reduce(): pl.pallas_call(functools.partial(reduce_kernel, n, rows, count), out_shap...]
    all_gather x6 -> x0, blocking collectives: 290 us -> none  [the longest x2 107 us: layer_backward(): lax.all_gather(jnp.transpose(deltas, (0, 2, 1)), 'seq', axis=1, tiled=True)]
    dot_general x50 -> x0, matrix products: 106 us -> none  [the longest x4 11.7 us: query_compute(): jnp.einsum('rhqk,rqhd->rkhd', score_grads, queries, preferred_element_typ...]
    unnamed x268 -> x58, local copies, waits for them, and re-layouts: 82 us -> 8.38 us
    psum x1 -> x0, blocking collectives: 44.4 us -> none  [shards(): total_squares = lax.psum(matrix_squares + vector_squares, ('seq', 'tp'))]
    convert_element_type x21 -> x9, other arithmetic: 43.3 us -> 4.83 us  [the longest x3 2.97 us: halves(): return values.astype(bf16).reshape(2, half, width)]
  transfers between devices with their start and end apart: 20 -> 0, of which waited for: 18 -> 0; matrix products, arithmetic and copies ran while one was open for 10% -> 0% of each run, Pallas kernels for 0% -> 0%
where the time goes in v1:
time: 427 us; the launch traced here: 423 us
  Pallas kernels  345 us (81%)
  local copies, waits for them, and re-layouts  35.5 us (8%)
  other arithmetic  35.4 us (8%)
  between operations  6.79 us (2%)
    pallas_call x3, Pallas kernels, reduce(): pl.pallas_call(functools.partial(reduce_kernel, n, rows, count), out_shap...  89.1 us
    pallas_call x3, Pallas kernels, gather(): pl.pallas_call(functools.partial(gather_kernel, n, rows, count), out_shap...  80.1 us
    pallas_call x1, Pallas kernels, spread(): pl.pallas_call(functools.partial(spread_kernel, n, rows), out_shape=(jax....  59.2 us
    pallas_call x1, Pallas kernels, collect(): pl.pallas_call(functools.partial(collect_kernel, n, rows), out_shape=(jax...  54.8 us
    pallas_call x2, Pallas kernels, backward(): pl.pallas_call(functools.partial(backward_kernel, batch, share, ff), out_...  30.8 us
    pallas_call x2, Pallas kernels, forward(): pl.pallas_call(functools.partial(forward_kernel, batch, share, ff), out_s...  21.6 us
    sub x5, other arithmetic, adam_update(): weight - rate * (first_hat / (jnp.sqrt(second_hat) + adam_eps) + decay *...  10.1 us
    pallas_call x1, Pallas kernels, share(): pl.pallas_call(functools.partial(share_kernel, n), out_shape=jax.ShapeDty...  9.36 us

profile of v1, /device:TPU:0, one launch (start us, length us, event | category | flops | bytes accessed | tf_op | source)
XLA Modules:
  0.0 422.6 jit_solution(14802703677389479774)
XLA Ops:
  0.7 2.4 pad_maximum_fusion.1.wide_ref
  10.1 59.2 %spread_inputs.1 = (f32[2,2,64,1024]{3,2,1,0:T(8,128)}, f32[16,16,128]{2,1,0:T(8,128)}, bf16[2,16,64,768]{3,2,1,0:T(8,128)(2,1)}) custom-call(f32[2,2,64,1024]{3,2,1,0:T(8,128)} %pad_maximum_fusion.1.wide_ref, f32[16,128]{1,0:T(8,128)} %pad.30.small_ref, bf16[2,8,64,768]{3,2,1,0:T(8,128)(2,1)} %pad_maximum_fusion.pack_ref), custom_call_target="tpu_custom_call" | custom-call | tf_op jit(solution)/shard_map/spread_inputs/pallas_call | solution.py:200
  74.0 34.0 %gather_tokens.3 = bf16[2,8,2,64,1024]{4,3,2,1,0:T(8,128)(2,1)} custom-call(bf16[2,2,64,1024]{3,2,1,0:T(8,128)(2,1)} %pad_maximum_fusion.3.x_ref), custom_call_target="tpu_custom_call" | custom-call | tf_op jit(solution)/shard_map/gather_tokens/pallas_call | solution.py:271
  108.0 5.1 %fusion.40 = (bf16[1,8,2,64,1024]{4,3,2,1,0:T(8,128)(2,1)}, bf16[1,8,2,64,1024]{4,3,2,1,0:T(8,128)(2,1)}) fusion(bf16[2,8,2,64,1024]{4,3,2,1,0:T(8,128)(2,1)} %gather_tokens.3), kind=kLoop, calls=%fused_computation.117 | loop fusion | bytes 8388608 | tf_op jit(solution)/shard_map/slice | solution.py:821
  113.1 1.9 fusion.41
  121.0 10.8 %layer_forward.2 = (bf16[1024,1024]{1,0:T(8,128)(2,1)}, bf16[1024,64]{1,0:T(8,128)(2,1)}, bf16[1024,64]{1,0:T(8,128)(2,1)}, bf16[1024,64]{1,0:T(8,128)(2,1)}, bf...) custom-call(bf16[1024,1024]{1,0:T(8,128)(2,1)} %bitcast.130, ...), custom_call_target="tpu_custom_call" | custom-call | tf_op jit(solution)/shard_map/layer_forward/pallas_call | solution.py:585
  131.8 26.9 %reduce_tokens.3 = f32[1,2,64,1024]{3,2,1,0:T(8,128)} custom-call(bf16[8,2,64,1024]{3,2,1,0:T(8,128)(2,1)} %bitcast.142), custom_call_target="tpu_custom_call" | custom-call | tf_op jit(solution)/shard_map/reduce_tokens/pallas_call | solution.py:342
  161.1 23.0 %gather_tokens.4 = bf16[1,8,2,64,1024]{4,3,2,1,0:T(8,128)(2,1)} custom-call(bf16[1,2,64,1024]{3,2,1,0:T(8,128)(2,1)} %get-tuple-element.138.x_ref), custom_call_target="tpu_custom_call" | custom-call | tf_op jit(solution)/shard_map/gather_tokens/pallas_call | solution.py:271
  184.2 10.8 %layer_forward.3 = (bf16[1024,1024]{1,0:T(8,128)(2,1)}, bf16[1024,64]{1,0:T(8,128)(2,1)}, bf16[1024,64]{1,0:T(8,128)(2,1)}, bf16[1024,64]{1,0:T(8,128)(2,1)}, bf...) custom-call(bf16[1024,1024]{1,0:T(8,128)(2,1)} %bitcast.128, ...), custom_call_target="tpu_custom_call" | custom-call | tf_op jit(solution)/shard_map/layer_forward/pallas_call | solution.py:585
  195.0 15.4 %layer_backward.2 = (bf16[1024,1024]{1,0:T(8,128)(2,1)}, bf16[1024,768]{1,0:T(8,128)(2,1)}) custom-call(bf16[1024,1024]{1,0:T(8,128)(2,1)} %bitcast.137, bf16[1024,1024]{1,0:T(8,128)(2,1)} %bitcast.129, bf16[1024,768]{1,0:T(8,128)(2,1)} %bitcast.135, f32[1024,128]{1,0:T(8,128)} %copy.56.cos_ref, f32[1024,128]{1,0:T(8,128)} %copy.57.sin_ref, ...), custom_call_target="tpu_custom_call" | custom-call | tf_op jit(solution)/shard_map/layer_backward/pallas_call | solution.py:658
  210.4 37.3 %reduce_tokens.4 = f32[2,2,64,1024]{3,2,1,0:T(8,128)} custom-call(bf16[8,2,64,1024]{3,2,1,0:T(8,128)(2,1)} %bitcast.143, bf16[8,2,64,1024]{3,2,1,0:T(8,128)(2,1)} %bitcast.144), custom_call_target="tpu_custom_call" | custom-call | tf_op jit(solution)/shard_map/reduce_tokens/pallas_call | solution.py:342
  249.0 1.9 fusion.17.x_ref
  250.9 23.1 %gather_tokens.5 = bf16[1,8,2,64,1024]{4,3,2,1,0:T(8,128)(2,1)} custom-call(bf16[1,2,64,1024]{3,2,1,0:T(8,128)(2,1)} %fusion.17.x_ref), custom_call_target="tpu_custom_call" | custom-call | tf_op jit(solution)/shard_map/gather_tokens/pallas_call | solution.py:271
  274.0 15.4 %layer_backward.3 = (bf16[1024,1024]{1,0:T(8,128)(2,1)}, bf16[1024,768]{1,0:T(8,128)(2,1)}) custom-call(bf16[1024,1024]{1,0:T(8,128)(2,1)} %bitcast.136, bf16[1024,1024]{1,0:T(8,128)(2,1)} %bitcast.131, bf16[1024,768]{1,0:T(8,128)(2,1)} %bitcast.133, f32[1024,128]{1,0:T(8,128)} %copy.56.cos_ref, f32[1024,128]{1,0:T(8,128)} %copy.57.sin_ref, ...), custom_call_target="tpu_custom_call" | custom-call | tf_op jit(solution)/shard_map/layer_backward/pallas_call | solution.py:658
  289.6 24.9 %reduce_tokens.5 = f32[1,2,64,1024]{3,2,1,0:T(8,128)} custom-call(bf16[8,2,64,1024]{3,2,1,0:T(8,128)(2,1)} %bitcast.141), custom_call_target="tpu_custom_call" | custom-call | tf_op jit(solution)/shard_map/reduce_tokens/pallas_call | solution.py:342
  319.4 54.8 %collect_gradients.1 = (bf16[2,8,64,768]{3,2,1,0:T(8,128)(2,1)}, f32[2,2,64,1024]{3,2,1,0:T(8,128)}, f32[16,8,128]{2,1,0:T(8,128)}) custom-call(bf16[16,64,768]{2,1,0:T(8,128)(2,1)} %bitcast.150, bf16[16,64,768]{2,1,0:T(8,128)(2,1)} %bitcast.149, f32[2,2,64,1024]{3,2,1,0:T(8,128)} %pad_maximum_fusion.2.refs_2_, f32[16,8,128]{2,1,0:T(8,128)} %pad.49.refs_3_), custom_call_target="tpu_custom_call" | custom-call | tf_op jit(solution)/shard_map/collect_gradients/pallas_call | solution.py:434
  374.2 2.4 slice_bitcast_fusion
  377.6 2.5 copy.69
  380.2 1.9 reshape.778
  390.7 9.4 %share_squares.1 = f32[32,8,128]{2,1,0:T(8,128)} custom-call(f32[8,128]{1,0:T(8,128)} %broadcast_in_dim.41.x_ref), custom_call_target="tpu_custom_call" | custom-call | tf_op jit(solution)/shard_map/share_squares/pallas_call | solution.py:479
  402.4 3.6 multiply_subtract_fusion.2
  407.0 2.0 multiply_subtract_fusion.3
  410.8 2.2 multiply_subtract_fusion.1
  414.6 2.2 multiply_subtract_fusion
  (138 shorter events, 42.6 us)
Async XLA Ops:
  0.7 2.5 copy-start.24
  0.7 2.5 copy-start.25
  0.7 2.5 copy-start.21
  0.7 3.2 copy-start.7
  0.7 3.2 copy-start.5
  4.0 1.6 copy-start.10
  69.2 3.5 copy-start
  107.9 5.1 %copy-start.9 = (bf16[2,16,64,768]{3,2,1,0:T(8,128)(2,1)S(1)}, bf16[2,16,64,768]{3,2,1,0:T(8,128)(2,1)}, u32[]{:S(2)}) copy-start(bf16[2,16,64,768]{3,2,1,0:T(8,128)(2,1)} %get-tuple-element.47) | copy-start | bytes 9437188
  158.8 1.5 copy-start.3
  274.0 15.4 %copy-start.1 = (f32[2,2,64,1024]{3,2,1,0:T(8,128)S(1)}, f32[2,2,64,1024]{3,2,1,0:T(8,128)}, u32[]{:S(2)}) copy-start(f32[2,2,64,1024]{3,2,1,0:T(8,128)} %reduce_tokens.4) | copy-start | bytes 3145732
  374.2 2.4 copy-start.4
  382.1 1.5 copy-start.2
  386.7 2.2 copy-start.20
  402.4 4.6 %copy-start.18 = (f32[2,64,512]{2,1,0:T(8,128)S(1)}, f32[2,64,512]{2,1,0:T(8,128)}, u32[]{:S(2)}) copy-start(f32[2,64,512]{2,1,0:T(8,128)} %param.29) | copy-start | bytes 786436
  402.4 4.6 %copy-start.19 = (f32[2,64,512]{2,1,0:T(8,128)S(1)}, f32[2,64,512]{2,1,0:T(8,128)}, u32[]{:S(2)}) copy-start(f32[2,64,512]{2,1,0:T(8,128)} %param.34) | copy-start | bytes 786436
  408.9 1.2 copy-start.14
  409.1 1.4 copy-start.6
  409.1 1.7 copy-start.13
  410.8 2.3 copy-start.16
  413.1 1.5 copy-start.15
  414.6 2.2 copy-start.22
  414.6 2.2 copy-start.23
  414.6 2.9 copy-start.12
  416.8 2.1 copy-start.11
  (2 other events, 2.2 us)
